TPU v7x, 32 devices: a whole 2x2x4 slice. The times are simulated.
32 devices in a mesh: gx: 4 (over y, core), gy: 8 (over z, x).
Axes of the slice: x: 2, y: 2, z: 4, core: 2. Of those that a mesh axis runs over, the one named last changes fastest.
Arguments:
- old_state: float32 [135, 8192], P(None, ('gx', 'gy')), as said below
- old_inverse: bfloat16 [135, 135, 8192], P(None, None, ('gx', 'gy'))
- old_start: int32 [32], replicated, may hold values from 0 to 5984, as said below
- neighbours: int32 [6, 6144], P(None, ('gx', 'gy')), may hold values from 0 to 6143, as said below
- orientation: int32 [6, 6144], P(None, ('gx', 'gy')), may hold values from 0 to 7, as said below
Outputs:
- new_state: float32 [135, 6144], P(None, ('gx', 'gy'))
- residual: float32 [135, 6144], P(None, ('gx', 'gy'))
Inputs may be any that keep to these rules, and one draw needn't show every extreme that they name: old_start[0] = 0 and each old_start[d] lies within 32 of d * 192; the last range ends at 6144; in every draw one device's old range holds exactly 256 elements, one start lies 32 below and another 32 above its new one, and the last start lies 32 above its new one. neighbours[f, e] names the element across face f of e; e is across face f xor 1 of that element. Device d holds elements d * 192 to (d + 1) * 192 - 1, with gx index d // 8 and gy index d % 8. The element across face 2k + h lies on e's own device, or for k = 0 on the device whose gx index is one lower (h = 0) or one higher (h = 1), cyclically, for k = 1 likewise along gy; for k = 2 it lies on e's own device. `orientation`: codes of the two sides of a face are inverse to one another. `old_state`: density lies in 0.5 to 1.8 and pressure in 0.5 to 1.8 at every node, padding slots included.
All inputs are finite; a program needn't handle non-finite values.
Results may differ from a plain program's by a relative error of at most 0.0003.
Values may be sent and summed in bfloat16 or wider, within the bound.
A program may use at most 128 MiB of HBM per device.

v0:
```python
import jax
import jax.numpy as jnp
from jax import lax
from jax.sharding import PartitionSpec as P

DIFF = [[-1.5, 2.0, -0.5], [-0.5, 0.0, 0.5], [0.5, -2.0, 1.5]]


def passed_along(value, axis, steps):
    count = lax.axis_size(axis)
    initial, last = (max(0, -steps), min(count, count - steps))
    return lax.ppermute(value, axis, [(source, source + steps) for source in range(initial, last)])


def padded(shard, sides, width):
    for axis, dim in sides:
        size, length = (lax.axis_size(axis), shard.shape[dim])
        up = [(i, (i + 1) % size) for i in range(size)]
        down = [(j, i) for i, j in up]
        last = lax.slice_in_dim(shard, length - width, length, axis=dim)
        initial = lax.slice_in_dim(shard, 0, width, axis=dim)
        before = lax.ppermute(last, axis, up)
        after = lax.ppermute(initial, axis, down)
        shard = jnp.concatenate([before, shard, after], axis=dim)
    return shard


def face_orderings():
    layout = [[p * 3 + q for q in range(3)] for p in range(3)]
    orderings = []
    for variant in range(8):
        arranged = layout
        if variant >= 4:
            arranged = [[layout[q][p] for q in range(3)] for p in range(3)]
        if variant % 2 == 1:
            arranged = arranged[::-1]
        if variant // 2 % 2 == 1:
            arranged = [entries[::-1] for entries in arranged]
        orderings.append([arranged[p][q] for p in range(3) for q in range(3)])
    return orderings


def reorient(neighbour_trace, orient_codes):
    result = jnp.zeros_like(neighbour_trace)
    for variant, ordering in enumerate(face_orderings()):
        result = result + jnp.where(orient_codes == variant, neighbour_trace[:, ordering, :], 0.0)
    return result


def euler_flux(conserved, axis_dim):
    density = conserved[0]
    velocity = conserved[1:4] / density
    pressure = 0.4 * (conserved[4] - 0.5 * jnp.sum(conserved[1:4] * velocity, axis=0))
    normal_vel = velocity[axis_dim]
    momentum = [conserved[1 + k] * normal_vel for k in range(3)]
    momentum[axis_dim] = momentum[axis_dim] + pressure
    fluxes = jnp.stack(
        [conserved[1 + axis_dim]] + momentum + [(conserved[4] + pressure) * normal_vel]
    )
    speed = jnp.abs(normal_vel) + jnp.sqrt(1.4 * pressure / density)
    return (fluxes, speed)


def derivative(values, axis_pos):
    planes = [lax.index_in_dim(values, j, axis_pos, keepdims=False) for j in range(3)]
    derived = [
        DIFF[i][0] * planes[0] + DIFF[i][1] * planes[1] + DIFF[i][2] * planes[2] for i in range(3)
    ]
    return jnp.stack(derived, axis=axis_pos)


def face_traces(conserved):
    columns = conserved.shape[-1]
    traces = []
    for face_id in range(6):
        traces.append(
            lax.index_in_dim(
                conserved, 2 * (face_id % 2), face_id // 2 + 1, keepdims=False
            ).reshape(5, 9, columns)
        )
    return jnp.stack(traces)


def dg_residual(flat, beyond):
    columns = flat.shape[-1]
    conserved = flat.reshape(5, 3, 3, 3, columns)
    residual = jnp.zeros_like(conserved)
    for axis_dim in range(3):
        residual = residual + derivative(euler_flux(conserved, axis_dim)[0], axis_dim + 1)
    for face_id in range(6):
        axis_dim = face_id // 2
        high_side = face_id % 2
        outward = 2.0 * high_side - 1.0
        inside = lax.index_in_dim(conserved, 2 * high_side, axis_dim + 1, keepdims=False)
        outside = beyond[face_id].reshape(inside.shape)
        flux_in, speed_in = euler_flux(inside, axis_dim)
        flux_out, speed_out = euler_flux(outside, axis_dim)
        wave_speed = jnp.maximum(speed_in, speed_out)
        common_flux = 0.5 * outward * (flux_in + flux_out) - 0.5 * wave_speed * (outside - inside)
        face_term = 3.0 * (common_flux - outward * flux_in)
        position = [slice(None)] * 5
        position[axis_dim + 1] = 2 * high_side
        residual = residual.at[tuple(position)].add(face_term)
    return residual.reshape(135, columns)


def move_states(slab, by):
    return passed_along(slab, ("gx", "gy"), by)


def move_blocks(slab, by):
    return passed_along(slab, ("gx", "gy"), by)


def hand_over(buffer, sender, range_start, range_end, device_id, elem_dev, margin):
    capacity = buffer.shape[-1]
    held = range_end - range_start
    lower_part = buffer[..., :margin]
    upper_part = lax.dynamic_slice_in_dim(buffer, held - margin, margin, buffer.ndim - 1)
    from_below = sender(upper_part, 1)
    from_above = sender(lower_part, -1)
    joined = jnp.concatenate([from_below, buffer, from_above], axis=-1)
    wanted = device_id * elem_dev + jnp.arange(elem_dev, dtype=jnp.int32)
    column = jnp.where(
        wanted < range_start,
        wanted - range_start + margin,
        jnp.where(
            wanted < range_end,
            margin + wanted - range_start,
            margin + capacity + wanted - range_end,
        ),
    )
    return jnp.take(joined, column, axis=-1)


def block_apply(inverse, vectors):
    return jnp.einsum(
        "ije,je->ie",
        inverse,
        vectors,
        precision=lax.Precision.HIGHEST,
        preferred_element_type=jnp.float32,
    )


def body(old_state, old_inverse, old_start, neighbours, orientation):
    devices = lax.axis_size(("gx", "gy"))
    device_id = lax.axis_index(("gx", "gy"))
    elem_dev = neighbours.shape[1]
    capacity = old_state.shape[1]
    margin = (capacity - elem_dev) // 2
    starts = jnp.concatenate([old_start, jnp.full((1,), devices * elem_dev, jnp.int32)])
    range_start = starts[device_id]
    range_end = starts[device_id + 1]
    conserved = hand_over(
        old_state, move_states, range_start, range_end, device_id, elem_dev, margin
    )
    traces = face_traces(conserved.reshape(5, 3, 3, 3, elem_dev))
    beyond = []
    tiles = padded(traces.reshape(1, 1, 270, elem_dev), (("gx", 0), ("gy", 1)), 1)
    tiles = tiles.reshape(9, 6, 45, elem_dev)
    size_gx = lax.axis_size("gx")
    size_gy = lax.axis_size("gy")
    row_gx = lax.axis_index("gx")
    row_gy = lax.axis_index("gy")
    for face_id in range(6):
        target = neighbours[face_id]
        owner_dev = target // elem_dev
        local_id = target % elem_dev
        step_gx = (owner_dev // size_gy - row_gx + 1) % size_gx
        step_gy = (owner_dev % size_gy - row_gy + 1) % size_gy
        tile_id = step_gx * 3 + step_gy
        flat_tiles = jnp.moveaxis(tiles[:, face_id ^ 1], 0, 1).reshape(45, 9 * elem_dev)
        neighbour_trace = jnp.take(flat_tiles, tile_id * elem_dev + local_id, axis=1).reshape(
            5, 9, elem_dev
        )
        beyond.append(reorient(neighbour_trace, orientation[face_id]))
    residual = dg_residual(conserved, beyond)
    inverse = hand_over(
        old_inverse, move_blocks, range_start, range_end, device_id, elem_dev, margin
    )
    update = block_apply(inverse, residual)
    return (conserved - update, residual)


def solution(mesh):
    placed = (
        P(None, ("gx", "gy")),
        P(None, None, ("gx", "gy")),
        P(),
        P(None, ("gx", "gy")),
        P(None, ("gx", "gy")),
    )
    return jax.shard_map(
        body,
        mesh=mesh,
        in_specs=placed,
        out_specs=(P(None, ("gx", "gy")), P(None, ("gx", "gy"))),
        check_vma=False,
    )
```

profile of v0, /device:TPU:0, one launch (start us, length us, event | category | flops | bytes accessed | tf_op | source)
XLA Modules:
  0.0 380.2 jit_solution(2211038254865158405)
XLA Ops:
  3.3 9.6 %constant_dynamic-slice_fusion = (bf16[135,135,32]{2,1,0:T(8,128)(2,1)}, bf16[135,135,32]{2,1,0:T(8,128)(2,1)}) fusion(bf16[135,135,256]{2,1,0:T(8,128)(2,1)} %param.68, s32[]{:T(128)S(6)} %select_n.889), kind=kLoop, calls=%fused_computation.734 | loop fusion | bytes 4665604 | tf_op jit(solution)/shard_map/dynamic_slice | solution.py:119
  13.0 6.3 %copy.807 = bf16[135,135,32]{1,2,0:T(8,128)(2,1)} copy(bf16[135,135,32]{2,1,0:T(8,128)(2,1)} %get-tuple-element.168) | data formatting | bytes 2332800
  19.4 7.6 %collective-permute-start.6 = (bf16[135,135,32]{1,2,0:T(8,128)(2,1)}, bf16[135,135,32]{1,2,0:T(8,128)(2,1)}, u32[]{:S(2)}, u32[]{:S(2)}) collective-permute-start(bf16[135,135,32]{1,2,0:T(8,128)(2,1)} %copy.807), channel_id=1, source_target_pairs={{0,1},{1,2},{2,3},{3,4},{4,5},{5,6},{6,7},{7,8},{8,9},{9,10},{10,1... | collective-permute-start | bytes 3499208 | tf_op jit(solution)/shard_map/ppermute | solution.py:12
  26.9 6.3 %copy.808 = bf16[135,135,32]{1,2,0:T(8,128)(2,1)} copy(bf16[135,135,32]{2,1,0:T(8,128)(2,1)} %get-tuple-element.169) | data formatting | bytes 2332800
  34.6 4.5 %collective-permute-start = (f32[135,32]{0,1:T(8,128)S(1)}, f32[135,32]{0,1:T(8,128)S(1)}, u32[]{:S(2)}, u32[]{:S(2)}) collective-permute-start(f32[135,32]{0,1:T(8,128)S(1)} %get-tuple-element.176), channel_id=1, source_target_pairs={{0,1},{1,2},{2,3},{3,4},{4,5},{5,6},{6,7},{7,8},{8,9},{9,10},{10,1... | collective-permute-start | bytes 51848 | tf_op jit(solution)/shard_map/ppermute | solution.py:12
  50.2 24.8 %copy.752 = bf16[135,135,256]{1,0,2:T(8,128)(2,1)} copy(bf16[135,135,256]{2,1,0:T(8,128)(2,1)} %param.68) | data formatting | bytes 18662400 | tf_op args[1]
  75.0 45.6 %collective-permute-done = f32[135,32]{0,1:T(8,128)S(1)} collective-permute-done((f32[135,32]{0,1:T(8,128)S(1)}, f32[135,32]{0,1:T(8,128)S(1)}, u32[]{:S(2)}, u32[]{:S(2)}) %collective-permute-start) | collective-permute-done | bytes 17312 | tf_op jit(solution)/shard_map/ppermute | solution.py:12
  120.6 5.2 %collective-permute-done.1 = f32[135,32]{0,1:T(8,128)S(1)} collective-permute-done((f32[135,32]{0,1:T(8,128)S(1)}, f32[135,32]{0,1:T(8,128)S(1)}, u32[]{:S(2)}, u32[]{:S(2)}) %collective-permute-start.1) | collective-permute-done | bytes 17312 | tf_op jit(solution)/shard_map/ppermute | solution.py:12
  130.8 1.7 collective-permute-start.3
  135.6 3.9 %collective-permute-done.2 = f32[1,1,270,192]{3,2,1,0:T(8,128)S(1)} collective-permute-done((f32[1,1,270,192]{3,2,1,0:T(8,128)S(1)}, f32[1,1,270,192]{3,2,1,0:T(8,128)S(1)}, u32[]{:S(2)}, u32[]{:S(2)}) %collective-permute-start.2) | collective-permute-done | bytes 207392 | tf_op jit(solution)/shard_map/ppermute | solution.py:22
  140.5 4.7 %collective-permute-start.5 = (f32[3,1,270,192]{3,1,2,0:T(1,128)S(1)}, f32[3,1,270,192]{3,1,2,0:T(1,128)S(1)}, u32[]{:S(2)}, u32[]{:S(2)}) collective-permute-start(f32[3,1,270,192]{3,1,2,0:T(1,128)S(1)} %copy.531), channel_id=1, source_target_pairs={{1,0},{2,1},{3,2},{4,3},{5,4},{6,5},{7,6},{0,7},{9,8},{10,9},{11,1... | collective-permute-start | bytes 1866248 | tf_op jit(solution)/shard_map/ppermute | solution.py:23
  146.5 30.0 %collective-permute-done.4 = f32[3,1,270,192]{3,1,2,0:T(1,128)S(1)} collective-permute-done((f32[3,1,270,192]{3,1,2,0:T(1,128)S(1)}, f32[3,1,270,192]{3,1,2,0:T(1,128)S(1)}, u32[]{:S(2)}, u32[]{:S(2)}) %collective-permute-start.4) | collective-permute-done | bytes 622112 | tf_op jit(solution)/shard_map/ppermute | solution.py:22
  176.5 2.4 collective-permute-done.5
  179.0 1.6 pad_maximum_fusion.1
  180.7 2.5 reshape.2694
  183.2 1.5 slice_bitcast_fusion
  184.7 1.4 copy.727
  243.8 1.5 maximum_multiply_fusion
  252.3 1.5 fusion.188
  264.9 1.4 slice.1163
  269.6 1.5 multiply_bitcast_fusion
  284.6 1.4 slice.1147
  289.3 1.5 multiply_bitcast_fusion.1
  301.7 1.4 multiply_bitcast_fusion.8
  303.1 1.4 stack.295
  311.3 1.5 scatter-add.26
  317.1 1.8 scatter-add.29
  319.9 2.9 copy.751
  322.7 4.3 %copy.753 = bf16[135,135,32]{1,0,2:T(8,128)(2,1)} copy(bf16[135,135,32]{1,2,0:T(8,128)(2,1)} %collective-permute-done.7) | data formatting | bytes 2332800 | tf_op jit(solution)/shard_map/ppermute | solution.py:12
  327.0 22.9 %pad_maximum_fusion = bf16[135,135,320]{1,0,2:T(8,128)(2,1)} fusion(bf16[135,135,32]{1,0,2:T(8,128)(2,1)} %copy.753, bf16[135,135,256]{1,0,2:T(8,128)(2,1)} %copy.752, bf16[135,135,32]{1,0,2:T(8,128)(2,1)S(1)} %copy.751), kind=kLoop, calls=%fused_computation.56 | loop fusion | flops 11664000 | bytes 23328000 | tf_op jit(solution)/shard_map/concatenate | solution.py:122
  349.9 16.2 %gather_fusion.49 = bf16[192,135,135]{2,1,0:T(8,128)(2,1)} fusion(bf16[135,135,320]{1,0,2:T(8,128)(2,1)} %pad_maximum_fusion, s32[1024]{0:T(1024)} %copy-done.42), kind=kCustom, calls=%fused_computation.55 | custom fusion | bytes 13997568 | tf_op jit(solution)/shard_map/jit(_take)/gather | solution.py:133
  366.1 13.2 %fusion = f32[192,1,135]{2,1,0:T(1,128)S(1)} fusion(f32[135,192,1]{0,2,1:T(1,128)S(1)} %copy.755, bf16[192,135,135]{2,1,0:T(8,128)(2,1)} %gather_fusion.49, pred[192]{0:T(512)(128)(4,1)S(1)} %copy-done.44), kind=kOutput, calls=%fused_computation.57 | convolution fusion | flops 45489600 | bytes 7205952 | tf_op jit(solution)/shard_map/ije,je->ie/dot_general | solution.py:137
  (398 shorter events, 142.6 us)
Async XLA Ops:
  19.4 300.5 %collective-permute-start.6 = (bf16[135,135,32]{1,2,0:T(8,128)(2,1)}, bf16[135,135,32]{1,2,0:T(8,128)(2,1)}, u32[]{:S(2)}, u32[]{:S(2)}) collective-permute-start(bf16[135,135,32]{1,2,0:T(8,128)(2,1)} %copy.807), channel_id=1, source_target_pairs={{0,1},{1,2},{2,3},{3,4},{4,5},{5,6},{6,7},{7,8},{8,9},{9,10},{10,1... | collective-permute-start | bytes 3499208 | tf_op jit(solution)/shard_map/ppermute | solution.py:12
  33.2 289.5 %collective-permute-start.7 = (bf16[135,135,32]{1,2,0:T(8,128)(2,1)}, bf16[135,135,32]{1,2,0:T(8,128)(2,1)}, u32[]{:S(2)}, u32[]{:S(2)}) collective-permute-start(bf16[135,135,32]{1,2,0:T(8,128)(2,1)} %copy.808), channel_id=1, source_target_pairs={{1,0},{2,1},{3,2},{4,3},{5,4},{6,5},{7,6},{8,7},{9,8},{10,9},{11,1... | collective-permute-start | bytes 3499208 | tf_op jit(solution)/shard_map/ppermute | solution.py:12
  34.6 85.9 %collective-permute-start = (f32[135,32]{0,1:T(8,128)S(1)}, f32[135,32]{0,1:T(8,128)S(1)}, u32[]{:S(2)}, u32[]{:S(2)}) collective-permute-start(f32[135,32]{0,1:T(8,128)S(1)} %get-tuple-element.176), channel_id=1, source_target_pairs={{0,1},{1,2},{2,3},{3,4},{4,5},{5,6},{6,7},{7,8},{8,9},{9,10},{10,1... | collective-permute-start | bytes 51848 | tf_op jit(solution)/shard_map/ppermute | solution.py:12
  39.2 86.6 %collective-permute-start.1 = (f32[135,32]{0,1:T(8,128)S(1)}, f32[135,32]{0,1:T(8,128)S(1)}, u32[]{:S(2)}, u32[]{:S(2)}) collective-permute-start(f32[135,32]{0,1:T(8,128)S(1)} %get-tuple-element.177), channel_id=1, source_target_pairs={{1,0},{2,1},{3,2},{4,3},{5,4},{6,5},{7,6},{8,7},{9,8},{10,9},{11,1... | collective-permute-start | bytes 51848 | tf_op jit(solution)/shard_map/ppermute | solution.py:12
  41.9 83.9 %copy-start.42 = (s32[1024]{0:T(1024)}, s32[1024]{0:T(1024)S(1)}, u32[]{:S(2)}) copy-start(s32[1024]{0:T(1024)S(1)} %pad_clamp_fusion.14) | copy-start | bytes 12292
  48.2 164.4 %copy-start.40 = (s32[1024]{0:T(1024)}, s32[1024]{0:T(1024)S(1)}, u32[]{:S(2)}) copy-start(s32[1024]{0:T(1024)S(1)} %get-tuple-element.361) | copy-start | bytes 12292
  48.2 165.0 %copy-start.39 = (s32[1024]{0:T(1024)}, s32[1024]{0:T(1024)S(1)}, u32[]{:S(2)}) copy-start(s32[1024]{0:T(1024)S(1)} %get-tuple-element.360) | copy-start | bytes 12292
  48.8 158.9 %copy-start.41 = (s32[1024]{0:T(1024)}, s32[1024]{0:T(1024)S(1)}, u32[]{:S(2)}) copy-start(s32[1024]{0:T(1024)S(1)} %get-tuple-element.358) | copy-start | bytes 12292
  50.2 78.7 %copy-start.43 = (pred[192]{0:T(512)(128)(4,1)}, pred[192]{0:T(512)(128)(4,1)S(1)}, u32[]{:S(2)}) copy-start(pred[192]{0:T(512)(128)(4,1)S(1)} %compare_and_fusion.6) | copy-start | bytes 580
  130.7 8.7 %collective-permute-start.2 = (f32[1,1,270,192]{3,2,1,0:T(8,128)S(1)}, f32[1,1,270,192]{3,2,1,0:T(8,128)S(1)}, u32[]{:S(2)}, u32[]{:S(2)}) collective-permute-start(f32[1,1,270,192]{3,2,1,0:T(8,128)S(1)} %reshape.2693), channel_id=1, source_target_pairs={{0,8},{8,16},{16,24},{24,0},{1,9},{9,17},{17,25},{25,1},{2,10},{10... | collective-permute-start | bytes 622088 | tf_op jit(solution)/shard_map/ppermute | solution.py:22
  130.8 8.7 %collective-permute-start.3 = (f32[1,1,270,192]{3,2,1,0:T(8,128)S(1)}, f32[1,1,270,192]{3,2,1,0:T(8,128)S(1)}, u32[]{:S(2)}, u32[]{:S(2)}) collective-permute-start(f32[1,1,270,192]{3,2,1,0:T(8,128)S(1)} %reshape.2693), channel_id=1, source_target_pairs={{8,0},{16,8},{24,16},{0,24},{9,1},{17,9},{25,17},{1,25},{10,2},{18... | collective-permute-start | bytes 622088 | tf_op jit(solution)/shard_map/ppermute | solution.py:23
  134.6 44.4 %copy-start.16 = (f32[3,3,3,192]{3,2,1,0:T(4,128)}, f32[3,3,3,192]{3,2,1,0:T(4,128)S(1)}, u32[]{:S(2)}) copy-start(f32[3,3,3,192]{3,2,1,0:T(4,128)S(1)} %get-tuple-element.165) | copy-start | bytes 62212
  134.6 44.4 %copy-start.17 = (f32[3,3,3,192]{3,2,1,0:T(4,128)}, f32[3,3,3,192]{3,2,1,0:T(4,128)S(1)}, u32[]{:S(2)}) copy-start(f32[3,3,3,192]{3,2,1,0:T(4,128)S(1)} %get-tuple-element.162) | copy-start | bytes 62212
  134.6 44.4 %copy-start.18 = (f32[3,3,3,192]{3,2,1,0:T(4,128)}, f32[3,3,3,192]{3,2,1,0:T(4,128)S(1)}, u32[]{:S(2)}) copy-start(f32[3,3,3,192]{3,2,1,0:T(4,128)S(1)} %get-tuple-element.164) | copy-start | bytes 62212
  134.6 44.4 %copy-start.19 = (f32[3,3,192]{2,1,0:T(4,128)}, f32[3,3,192]{2,1,0:T(4,128)S(1)}, u32[]{:S(2)}) copy-start(f32[3,3,192]{2,1,0:T(4,128)S(1)} %get-tuple-element.84) | copy-start | bytes 20740
  134.6 44.4 %copy-start.20 = (f32[3,3,192]{2,1,0:T(4,128)}, f32[3,3,192]{2,1,0:T(4,128)S(1)}, u32[]{:S(2)}) copy-start(f32[3,3,192]{2,1,0:T(4,128)S(1)} %get-tuple-element.83) | copy-start | bytes 20740
  134.7 48.4 %copy-start.24 = (f32[5,3,1,3,192]{4,3,1,2,0:T(4,128)}, f32[5,3,1,3,192]{4,3,1,2,0:T(4,128)S(1)}, u32[]{:S(2)}) copy-start(f32[5,3,1,3,192]{4,3,1,2,0:T(4,128)S(1)} %get-tuple-element.199) | copy-start | bytes 103684
  134.7 48.4 %copy-start.29 = (f32[5,3,1,3,192]{4,3,1,2,0:T(4,128)}, f32[5,3,1,3,192]{4,3,1,2,0:T(4,128)S(1)}, u32[]{:S(2)}) copy-start(f32[5,3,1,3,192]{4,3,1,2,0:T(4,128)S(1)} %constant_dynamic-update-slice_fusion.38) | copy-start | bytes 103684
  140.4 36.0 %collective-permute-start.4 = (f32[3,1,270,192]{3,1,2,0:T(1,128)S(1)}, f32[3,1,270,192]{3,1,2,0:T(1,128)S(1)}, u32[]{:S(2)}, u32[]{:S(2)}) collective-permute-start(f32[3,1,270,192]{3,1,2,0:T(1,128)S(1)} %copy.531), channel_id=1, source_target_pairs={{0,1},{1,2},{2,3},{3,4},{4,5},{5,6},{6,7},{7,0},{8,9},{9,10},{10,1... | collective-permute-start | bytes 1866248 | tf_op jit(solution)/shard_map/ppermute | solution.py:22
  140.5 38.4 %collective-permute-start.5 = (f32[3,1,270,192]{3,1,2,0:T(1,128)S(1)}, f32[3,1,270,192]{3,1,2,0:T(1,128)S(1)}, u32[]{:S(2)}, u32[]{:S(2)}) collective-permute-start(f32[3,1,270,192]{3,1,2,0:T(1,128)S(1)} %copy.531), channel_id=1, source_target_pairs={{1,0},{2,1},{3,2},{4,3},{5,4},{6,5},{7,6},{0,7},{9,8},{10,9},{11,1... | collective-permute-start | bytes 1866248 | tf_op jit(solution)/shard_map/ppermute | solution.py:23
  145.2 38.0 %copy-start.37 = (f32[5,3,3,1,192]{4,3,2,1,0:T(1,128)}, f32[5,3,3,1,192]{4,3,2,1,0:T(1,128)S(1)}, u32[]{:S(2)}) copy-start(f32[5,3,3,1,192]{4,3,2,1,0:T(1,128)S(1)} %constant_dynamic-update-slice_fusion.58) | copy-start | bytes 103684
  230.9 43.8 %copy-start.4 = (f32[9,5,192]{2,1,0:T(8,128)S(1)}, f32[9,5,192]{2,1,0:T(8,128)}, u32[]{:S(2)}) copy-start(f32[9,5,192]{2,1,0:T(8,128)} %gather_fusion.8) | copy-start | bytes 103684
  230.9 43.8 %copy-start.5 = (f32[9,5,192]{2,1,0:T(8,128)S(1)}, f32[9,5,192]{2,1,0:T(8,128)}, u32[]{:S(2)}) copy-start(f32[9,5,192]{2,1,0:T(8,128)} %gather_fusion.3) | copy-start | bytes 103684
  234.5 45.6 %copy-start.45 = (pred[192]{0:T(512)(128)(4,1)S(1)}, pred[192]{0:T(512)(128)(4,1)}, u32[]{:S(2)}) copy-start(pred[192]{0:T(512)(128)(4,1)} %get-tuple-element.104) | copy-start | bytes 580
  237.8 78.2 %copy-start.6 = (f32[9,5,192]{2,1,0:T(8,128)S(1)}, f32[9,5,192]{2,1,0:T(8,128)}, u32[]{:S(2)}) copy-start(f32[9,5,192]{2,1,0:T(8,128)} %gather_fusion.41) | copy-start | bytes 103684
  237.8 78.2 %copy-start.7 = (f32[9,5,192]{2,1,0:T(8,128)S(1)}, f32[9,5,192]{2,1,0:T(8,128)}, u32[]{:S(2)}) copy-start(f32[9,5,192]{2,1,0:T(8,128)} %gather_fusion.42) | copy-start | bytes 103684
  237.8 78.2 %copy-start.8 = (f32[9,5,192]{2,1,0:T(8,128)S(1)}, f32[9,5,192]{2,1,0:T(8,128)}, u32[]{:S(2)}) copy-start(f32[9,5,192]{2,1,0:T(8,128)} %gather_fusion.43) | copy-start | bytes 103684
  237.8 78.2 %copy-start.9 = (f32[9,5,192]{2,1,0:T(8,128)S(1)}, f32[9,5,192]{2,1,0:T(8,128)}, u32[]{:S(2)}) copy-start(f32[9,5,192]{2,1,0:T(8,128)} %gather_fusion.44) | copy-start | bytes 103684
  237.8 78.2 %copy-start.10 = (f32[9,5,192]{2,1,0:T(8,128)S(1)}, f32[9,5,192]{2,1,0:T(8,128)}, u32[]{:S(2)}) copy-start(f32[9,5,192]{2,1,0:T(8,128)} %gather_fusion.45) | copy-start | bytes 103684
  237.9 78.2 %copy-start.11 = (f32[9,5,192]{2,1,0:T(8,128)S(1)}, f32[9,5,192]{2,1,0:T(8,128)}, u32[]{:S(2)}) copy-start(f32[9,5,192]{2,1,0:T(8,128)} %gather_fusion.46) | copy-start | bytes 103684
  237.9 78.2 %copy-start.12 = (f32[9,5,192]{2,1,0:T(8,128)S(1)}, f32[9,5,192]{2,1,0:T(8,128)}, u32[]{:S(2)}) copy-start(f32[9,5,192]{2,1,0:T(8,128)} %gather_fusion.47) | copy-start | bytes 103684
  237.9 78.2 %copy-start.13 = (f32[9,5,192]{2,1,0:T(8,128)S(1)}, f32[9,5,192]{2,1,0:T(8,128)}, u32[]{:S(2)}) copy-start(f32[9,5,192]{2,1,0:T(8,128)} %gather_fusion.48) | copy-start | bytes 103684
  (33 other events, 570.2 us)
where the time goes:
time: 385 us; the launch traced here: 380 us
  local copies, waits for them, and re-layouts  173 us (45%)
  waiting for transfers between devices  87 us (23%)
  other arithmetic  82.1 us (21%)
  starting transfers between devices  21.2 us (6%)
  matrix products  13.2 us (3%)
    ppermute x4, waiting for transfers between devices, passed_along(): lax.ppermute(value, axis, [(source, source + steps) for source in range(i...  50.8 us
    unnamed x148, local copies, waits for them, and re-layouts  46.2 us
    gather x48, local copies, waits for them, and re-layouts, reorient(): neighbour_trace[:, ordering, :]  39.9 us
    ppermute x2, waiting for transfers between devices, padded(): before = lax.ppermute(last, axis, up)  33.8 us
    concatenate x2, other arithmetic, hand_over(): joined = jnp.concatenate([from_below, buffer, from_above], axis=-1)  22.9 us
    gather x4, local copies, waits for them, and re-layouts, hand_over(): return jnp.take(joined, column, axis=-1)  17.2 us
    ppermute x4, starting transfers between devices, passed_along(): lax.ppermute(value, axis, [(source, source + steps) for source in range(i...  14.7 us
    dot_general x1, matrix products, block_apply(): jnp.einsum('ije,je->ie', inverse, vectors, precision=lax.Precision.HIGHES...  13.2 us
  transfers between devices with their start and end apart: 8, of which 5 were waited for; matrix products, arithmetic and copies ran while one was open for 50% of the time, Pallas kernels for 0%

commit v1 on v0

v1 whole, which is shorter than its diff:
```python
import numpy as np
import jax
import jax.numpy as jnp
from jax import lax
from jax.experimental import pallas as pl
from jax.experimental.pallas import tpu as pltpu
from jax.sharding import PartitionSpec as P

DIFF = np.array([[-1.5, 2.0, -0.5], [-0.5, 0.0, 0.5], [0.5, -2.0, 1.5]])
MESH = pl.DeviceIdType.MESH
NODES = 27
ROWS = 135
FACE_ROWS = 48
CHUNKS = 5


def face_node(face, position):
    k, h = face // 2, face % 2
    other = [position // 3, position % 3]
    index = other[:k] + [2 * h] + other[k:]
    return 9 * index[0] + 3 * index[1] + index[2]


def selections():
    send = np.zeros((6 * FACE_ROWS, ROWS), np.float32)
    inside = np.zeros((72, NODES), np.float32)
    lift = np.zeros((NODES, 72), np.float32)
    for face in range(6):
        for position in range(9):
            node = face_node(face, position)
            for v in range(5):
                send[face * FACE_ROWS + v * 9 + position, v * NODES + node] = 1.0
            inside[position * 8 + face, node] = 1.0
            lift[node, position * 8 + face] = 1.0
    eye = np.eye(3)
    along = np.concatenate(
        [
            np.kron(np.kron(DIFF, eye), eye),
            np.kron(np.kron(eye, DIFF), eye),
            np.kron(np.kron(eye, eye), DIFF),
        ],
        axis=1,
    ).astype(np.float32)
    thrice = lambda m: np.concatenate([m, m, m], axis=1)
    return [jnp.asarray(thrice(m), jnp.bfloat16) for m in (send, inside, along, lift)]


def parts_of(x):
    high = x.astype(jnp.bfloat16)
    rest = x - high.astype(jnp.float32)
    mid = rest.astype(jnp.bfloat16)
    low = (rest - mid.astype(jnp.float32)).astype(jnp.bfloat16)
    return [high, mid, low]


def times(matrix, x):
    return jnp.dot(
        matrix, jnp.concatenate(parts_of(x), axis=0), preferred_element_type=jnp.float32
    )


def pressure_of(u, inverse_density):
    kinetic = (u[1] * u[1] + u[2] * u[2] + u[3] * u[3]) * inverse_density
    return 0.4 * (u[4] - 0.5 * kinetic)


def kernel(
    n_gx, n_gy,
    state_ref, inverse_ref, start_ref, neigh_ref, orient_ref,
    send_mat, inside_mat, along_mat, lift_mat,
    new_ref, residual_ref,
    block_ref, view_ref, edge_prev, edge_next,
    traces_ref, far_ref, out_ref, res_ref, res_prev, res_next,
    old_res, upd_ref, upd_prev, upd_next, index_ref, code_ref,
    load_sem, send_sem, recv_sem,
):
    elems = neigh_ref.shape[1]
    capacity = state_ref.shape[1]
    half = capacity // 2
    count = n_gx * n_gy
    gx = lax.axis_index("gx")
    gy = lax.axis_index("gy")
    me = gx * n_gy + gy

    after = lax.rem(me + 1, count)
    before = lax.rem(me + count - 1, count)
    nxt = (after // n_gy, lax.rem(after, n_gy))
    prv = (before // n_gy, lax.rem(before, n_gy))
    sides = [
        (lax.rem(gx + n_gx - 1, n_gx), gy),
        (lax.rem(gx + 1, n_gx), gy),
        (gx, lax.rem(gy + n_gy - 1, n_gy)),
        (gx, lax.rem(gy + 1, n_gy)),
    ]

    barrier = pltpu.get_barrier_semaphore()
    for device in [nxt, prv] + sides:
        pl.semaphore_signal(barrier, inc=1, device_id=device, device_id_type=MESH)

    rows = ROWS // CHUNKS
    loads = []
    for chunk in range(CHUNKS):
        where = pl.ds(chunk * rows, rows)
        load = pltpu.make_async_copy(
            inverse_ref.at[where], block_ref.at[where], load_sem.at[chunk]
        )
        load.start()
        loads.append(load)

    def send(slot, source, target, device):
        copy = pltpu.make_async_remote_copy(
            src_ref=source, dst_ref=target, send_sem=send_sem.at[slot],
            recv_sem=recv_sem.at[slot], device_id=device, device_id_type=MESH,
        )
        copy.start()
        return copy

    start = start_ref[me]
    end = jnp.where(me == count - 1, count * elems, start_ref[lax.rem(me + 1, count)])
    held = end - start
    shift = me * elems - start
    to_new = jnp.where(shift > 0, capacity - shift, -shift)
    to_old = jnp.where(shift >= 0, shift, capacity + shift)

    view_ref[...] = pltpu.roll(state_ref[...], to_new, 1)
    pl.semaphore_wait(barrier, 6)
    edge = view_ref.at[:, pl.ds(half, half)]
    copies = [send(0, edge, edge_prev, nxt), send(1, edge, edge_next, prv)]

    index_ref[...] = jnp.zeros_like(index_ref)
    code_ref[...] = jnp.zeros_like(code_ref)
    index_ref[0:6, 0:elems] = neigh_ref[...]
    code_ref[0:6, 0:elems] = orient_ref[...]
    choices = []
    for face in range(6):
        local = index_ref[face : face + 1, :] - me * elems
        if face < 4:
            own = jnp.logical_and(local >= 0, local < elems)
            other = sides[face][0] * n_gy + sides[face][1]
            local = jnp.where(own, local, capacity + local + (me - other) * elems)
        width = capacity * (2 if face < 4 else 1)
        columns = lax.broadcasted_iota(jnp.int32, (width, capacity), 0)
        choices.append(jnp.where(columns == local, 1.0, 0.0).astype(jnp.bfloat16))

    lane = lax.broadcasted_iota(jnp.int32, (1, half), 1)

    def merged(ref, from_prev, from_next):
        low = jnp.where(lane + shift < 0, pltpu.roll(from_prev[...], half // 2, 1), ref[:, 0:half])
        high = jnp.where(
            lane + half + shift >= held, pltpu.roll(from_next[...], half // 2, 1), ref[:, half:]
        )
        return low, high

    for copy in copies:
        copy.wait()
    low, high = merged(view_ref, edge_prev, edge_next)
    high = jnp.where(lane + half < elems, high, 0.0)
    view_ref[:, 0:half] = low
    view_ref[:, half:] = high
    state = view_ref[...]

    traces_ref[...] = times(send_mat[...], state)
    copies = []
    for face in range(4):
        copies.append(
            send(
                2 + face,
                traces_ref.at[pl.ds(face * FACE_ROWS, FACE_ROWS)],
                far_ref.at[pl.ds(face * FACE_ROWS, FACE_ROWS)],
                sides[face],
            )
        )

    u = [view_ref[NODES * v : NODES * (v + 1), :] for v in range(5)]
    inverse_density = 1.0 / u[0]
    pressure = pressure_of(u, inverse_density)
    flux = [[] for _ in range(5)]
    for k in range(3):
        velocity = u[1 + k] * inverse_density
        flux[0].append(u[1 + k])
        for j in range(3):
            value = u[1 + j] * velocity
            flux[1 + j].append(value + pressure if j == k else value)
        flux[4].append((u[4] + pressure) * velocity)
    volume = [times(along_mat[...], jnp.concatenate(flux[v], axis=0)) for v in range(5)]
    inside = [times(inside_mat[...], u[v]).reshape(9, 8, capacity) for v in range(5)]

    for face in range(4):
        copies[face].wait()

    out_ref[...] = jnp.zeros_like(out_ref)
    for face in range(6):
        where = pl.ds((face ^ 1) * FACE_ROWS, FACE_ROWS)
        block = traces_ref[where, :]
        if face < 4:
            block = jnp.concatenate([block, far_ref[where, :]], axis=1)
        pieces = jnp.dot(
            jnp.concatenate(parts_of(block), axis=0), choices[face],
            preferred_element_type=jnp.float32,
        )
        taken = pieces[0:48] + pieces[48:96] + pieces[96:144]
        out_ref[:, face, :] = taken[0:45]

    code = code_ref[...]
    swapped = code >= 4
    flip_p = (code & 1) == 1
    flip_q = (code & 2) == 2
    outside = []
    for v in range(5):
        t = [[out_ref[9 * v + 3 * p + q] for q in range(3)] for p in range(3)]
        t = [[jnp.where(swapped, t[q][p], t[p][q]) if p != q else t[p][q] for q in range(3)] for p in range(3)]
        t = [[jnp.where(flip_p, t[2 - p][q], t[p][q]) if p != 1 else t[p][q] for q in range(3)] for p in range(3)]
        t = [[jnp.where(flip_q, t[p][2 - q], t[p][q]) if q != 1 else t[p][q] for q in range(3)] for p in range(3)]
        outside.append(jnp.stack([t[p][q] for p in range(3) for q in range(3)]))

    face_of = lax.broadcasted_iota(jnp.int32, (1, 8, capacity), 1)
    real = face_of < 6
    outward = jnp.where((face_of & 1) == 1, 1.0, -1.0)
    normal = [jnp.logical_and(face_of >= 2 * k, face_of < 2 * k + 2) for k in range(3)]

    def normal_flux(w):
        inverse_density = 1.0 / w[0]
        pressure = pressure_of(w, inverse_density)
        momentum = jnp.where(normal[0], w[1], jnp.where(normal[1], w[2], w[3]))
        velocity = momentum * inverse_density
        values = [momentum]
        for j in range(3):
            values.append(w[1 + j] * velocity + jnp.where(normal[j], pressure, 0.0))
        values.append((w[4] + pressure) * velocity)
        return values, jnp.abs(velocity) + jnp.sqrt(1.4 * pressure * inverse_density)

    flux_in, speed_in = normal_flux(inside)
    flux_out, speed_out = normal_flux(outside)
    speed = jnp.maximum(speed_in, speed_out)
    for v in range(5):
        term = 1.5 * (outward * (flux_out[v] - flux_in[v]) - speed * (outside[v] - inside[v]))
        term = jnp.where(real, term, 0.0).reshape(72, capacity)
        res_ref[NODES * v : NODES * (v + 1), :] = volume[v] + times(lift_mat[...], term)

    copies = [
        send(6, res_ref.at[:, pl.ds(0, half)], res_next, prv),
        send(7, res_ref.at[:, pl.ds(half, half)], res_prev, nxt),
    ]
    residual_ref[...] = res_ref[:, 0:elems]
    for copy in copies:
        copy.wait()
    quarter = half // 2
    inner = lane < elems - half
    to_next = lane < elems - half + quarter // 2
    high = jnp.where(
        inner, res_ref[:, half:],
        jnp.where(to_next, pltpu.roll(res_next[...], quarter, 1), pltpu.roll(res_prev[...], quarter, 1)),
    )
    old_res[...] = pltpu.roll(jnp.concatenate([res_ref[:, 0:half], high], axis=1), to_old, 1)

    for chunk in range(CHUNKS):
        loads[chunk].wait()

        def apply(step, carry):
            for t in range(3):
                row = chunk * rows + step * 3 + t
                product = block_ref[row].astype(jnp.float32) * old_res[...]
                upd_ref[pl.ds(row, 1), :] = jnp.sum(product, axis=0, keepdims=True)
            return carry

        lax.fori_loop(0, rows // 3, apply, 0)

    upd_ref[...] = pltpu.roll(upd_ref[...], to_new, 1)
    edge = upd_ref.at[:, pl.ds(half, half)]
    copies = [send(8, edge, upd_prev, nxt), send(9, edge, upd_next, prv)]
    for copy in copies:
        copy.wait()
    low, high = merged(upd_ref, upd_prev, upd_next)
    new_ref[:, 0:half] = view_ref[:, 0:half] - low
    new_ref[:, half:elems] = (view_ref[:, half:] - high)[:, 0 : elems - half]


def solution(mesh):
    n_gx, n_gy = mesh.shape["gx"], mesh.shape["gy"]

    def body(old_state, old_inverse, old_start, neighbours, orientation):
        elems, capacity = neighbours.shape[1], old_state.shape[1]
        half = capacity // 2
        vmem = pl.BlockSpec(memory_space=pltpu.VMEM)
        f32 = lambda *shape: pltpu.VMEM(shape, jnp.float32)
        call = pl.pallas_call(
            lambda *refs: kernel(n_gx, n_gy, *refs),
            out_shape=[jax.ShapeDtypeStruct((ROWS, elems), jnp.float32)] * 2,
            in_specs=[
                vmem,
                pl.BlockSpec(memory_space=pl.ANY),
                pl.BlockSpec(memory_space=pltpu.SMEM),
                vmem, vmem, vmem, vmem, vmem, vmem,
            ],
            out_specs=[vmem, vmem],
            scratch_shapes=[
                pltpu.VMEM((ROWS, ROWS, capacity), jnp.bfloat16),
                f32(ROWS, capacity), f32(ROWS, half), f32(ROWS, half),
                f32(6 * FACE_ROWS, capacity), f32(4 * FACE_ROWS, capacity),
                f32(45, 8, capacity),
                f32(ROWS, capacity), f32(ROWS, half), f32(ROWS, half),
                f32(ROWS, capacity),
                f32(ROWS, capacity), f32(ROWS, half), f32(ROWS, half),
                pltpu.VMEM((8, capacity), jnp.int32), pltpu.VMEM((8, capacity), jnp.int32),
                pltpu.SemaphoreType.DMA((CHUNKS,)),
                pltpu.SemaphoreType.DMA((10,)),
                pltpu.SemaphoreType.DMA((10,)),
            ],
            compiler_params=pltpu.CompilerParams(
                collective_id=0, has_side_effects=True, vmem_limit_bytes=48 * 1024 * 1024
            ),
        )
        return tuple(call(old_state, old_inverse, old_start, neighbours, orientation, *selections()))

    spread = P(None, ("gx", "gy"))
    return jax.shard_map(
        body,
        mesh=mesh,
        in_specs=(spread, P(None, None, ("gx", "gy")), P(), spread, spread),
        out_specs=(spread, spread),
        check_vma=False,
    )
```

time: 385 us -> 39 us (0.10); the launches traced: 380 us -> 38.5 us
  local copies, waits for them, and re-layouts: 173 us -> 7.39 us
  waiting for transfers between devices: 87 us -> 0 us
  other arithmetic: 82.1 us -> 0 us
  Pallas kernels: 0 us -> 30.5 us
  starting transfers between devices: 21.2 us -> 0 us
  matrix products: 13.2 us -> 0 us
    ppermute x8 -> x0, waiting for transfers between devices: 87 us -> none  [the longest x4 50.8 us: passed_along(): lax.ppermute(value, axis, [(source, source + steps) for source in range(i...]
    gather x58 -> x0, local copies, waits for them, and re-layouts: 62.4 us -> none  [the longest x48 39.9 us: reorient(): neighbour_trace[:, ordering, :]]
    unnamed x148 -> x18, local copies, waits for them, and re-layouts: 46.2 us -> 7.39 us
    pallas_call x0 -> x1, Pallas kernels: none -> 30.5 us  [body(): call(old_state, old_inverse, old_start, neighbours, orientation, *selecti...]
    concatenate x4 -> x0, other arithmetic: 25.3 us -> none  [the longest x2 22.9 us: hand_over(): joined = jnp.concatenate([from_below, buffer, from_above], axis=-1)]
    ppermute x8 -> x0, starting transfers between devices: 21.2 us -> none  [the longest x4 14.7 us: passed_along(): lax.ppermute(value, axis, [(source, source + steps) for source in range(i...]
    slice x23 -> x0, local copies, waits for them, and re-layouts: 14 us -> none  [the longest x8 7.64 us: euler_flux(): momentum = [conserved[1 + k] * normal_vel for k in range(3)]]
    dot_general x1 -> x0, matrix products: 13.2 us -> none  [block_apply(): jnp.einsum('ije,je->ie', inverse, vectors, precision=lax.Precision.HIGHES...]
  transfers between devices with their start and end apart: 8 -> 0, of which waited for: 5 -> 0; matrix products, arithmetic and copies ran while one was open for 50% -> 0% of each run, Pallas kernels for 0% -> 0%
where the time goes in v1:
time: 39 us; the launch traced here: 38.5 us
  Pallas kernels  30.5 us (78%)
  local copies, waits for them, and re-layouts  7.39 us (19%)
  between operations  0.66 us (2%)
    pallas_call x1, Pallas kernels, body(): call(old_state, old_inverse, old_start, neighbours, orientation, *selecti...  30.5 us
    unnamed x18, local copies, waits for them, and re-layouts  7.39 us

profile of v1, /device:TPU:0, one launch (start us, length us, event | category | flops | bytes accessed | tf_op | source)
XLA Modules:
  0.0 38.5 jit_solution(12503820550432744458)
XLA Ops:
  0.6 0.0 copy-start
  0.6 1.0 %copy-done = bf16[288,405]{1,0:T(8,128)(2,1)S(1)} copy-done((bf16[288,405]{1,0:T(8,128)(2,1)S(1)}, bf16[288,405]{1,0:T(8,128)(2,1)}, u32[]{:S(2)}) %copy-start) | copy-done | bytes 233304
  1.6 0.0 copy-start.1
  1.6 0.9 %copy-done.1 = f32[135,256]{1,0:T(8,128)S(1)} copy-done((f32[135,256]{1,0:T(8,128)S(1)}, f32[135,256]{1,0:T(8,128)}, u32[]{:S(2)}) %copy-start.1) | copy-done | bytes 138264
  2.5 0.0 copy-start.2
  2.5 0.7 %copy-done.2 = bf16[72,81]{1,0:T(8,128)(2,1)S(1)} copy-done((bf16[72,81]{1,0:T(8,128)(2,1)S(1)}, bf16[72,81]{1,0:T(8,128)(2,1)}, u32[]{:S(2)}) %copy-start.2) | copy-done | bytes 11688
  3.2 0.0 copy-start.3
  3.2 0.7 %copy-done.3 = bf16[27,216]{1,0:T(8,128)(2,1)S(1)} copy-done((bf16[27,216]{1,0:T(8,128)(2,1)S(1)}, bf16[27,216]{1,0:T(8,128)(2,1)}, u32[]{:S(2)}) %copy-start.3) | copy-done | bytes 11688
  3.9 0.0 copy-start.4
  3.9 0.7 %copy-done.4 = bf16[27,243]{1,0:T(8,128)(2,1)S(1)} copy-done((bf16[27,243]{1,0:T(8,128)(2,1)S(1)}, bf16[27,243]{1,0:T(8,128)(2,1)}, u32[]{:S(2)}) %copy-start.4) | copy-done | bytes 13146
  4.7 0.0 copy-start.5
  4.7 0.7 %copy-done.5 = s32[6,192]{1,0:T(8,128)S(1)} copy-done((s32[6,192]{1,0:T(8,128)S(1)}, s32[6,192]{1,0:T(8,128)}, u32[]{:S(2)}) %copy-start.5) | copy-done | bytes 4632
  5.4 0.0 copy-start.6
  5.4 0.7 %copy-done.6 = s32[6,192]{1,0:T(8,128)S(1)} copy-done((s32[6,192]{1,0:T(8,128)S(1)}, s32[6,192]{1,0:T(8,128)}, u32[]{:S(2)}) %copy-start.6) | copy-done | bytes 4632
  6.1 0.0 copy-start.7
  6.1 0.7 %copy-done.7 = s32[32]{0:T(128)S(1)} copy-done((s32[32]{0:T(128)S(1)}, s32[32]{0:T(128)}, u32[]{:S(2)}) %copy-start.7) | copy-done | bytes 152
  6.7 30.5 %shard_map.104 = (f32[135,192]{1,0:T(8,128)S(1)}, f32[135,192]{1,0:T(8,128)S(1)}) custom-call(f32[135,256]{1,0:T(8,128)S(1)} %copy-done.1, bf16[135,135,256]{2,1,0:T(8,128)(2,1)} %refs_1_.1, s32[32]{0:T(128)S(1)} %copy-done.7, s32[6,192]{1,0:T(8,128)S(1)} %copy-done.5, s32[6,192]{1,0:T(8,128)S(1)} %copy-done.6, bf16[288,405]{1,0:T(8,128)(2,1)S(1)} %copy-done, ...), custom_call_target="tpu_custom_call" | custom-call | tf_op jit(solution)/shard_map/pallas_call | solution.py:313
  37.2 0.7 %copy.13 = f32[135,192]{1,0:T(8,128)} copy(f32[135,192]{1,0:T(8,128)S(1)} %get-tuple-element.4) | data formatting | bytes 207360
  37.9 0.7 %copy.14 = f32[135,192]{1,0:T(8,128)} copy(f32[135,192]{1,0:T(8,128)S(1)} %get-tuple-element.5) | data formatting | bytes 207360
Async XLA Ops:
  0.6 1.0 %copy-start = (bf16[288,405]{1,0:T(8,128)(2,1)S(1)}, bf16[288,405]{1,0:T(8,128)(2,1)}, u32[]{:S(2)}) copy-start(bf16[288,405]{1,0:T(8,128)(2,1)} %constant.8.clone.refs_5_) | copy-start | bytes 699844
  1.6 0.9 %copy-start.1 = (f32[135,256]{1,0:T(8,128)S(1)}, f32[135,256]{1,0:T(8,128)}, u32[]{:S(2)}) copy-start(f32[135,256]{1,0:T(8,128)} %refs_0_.1) | copy-start | bytes 414724
  2.5 0.7 %copy-start.2 = (bf16[72,81]{1,0:T(8,128)(2,1)S(1)}, bf16[72,81]{1,0:T(8,128)(2,1)}, u32[]{:S(2)}) copy-start(bf16[72,81]{1,0:T(8,128)(2,1)} %constant.9.clone.refs_6_) | copy-start | bytes 34996
  3.2 0.7 %copy-start.3 = (bf16[27,216]{1,0:T(8,128)(2,1)S(1)}, bf16[27,216]{1,0:T(8,128)(2,1)}, u32[]{:S(2)}) copy-start(bf16[27,216]{1,0:T(8,128)(2,1)} %constant.11.clone.refs_8_) | copy-start | bytes 34996
  3.9 0.7 %copy-start.4 = (bf16[27,243]{1,0:T(8,128)(2,1)S(1)}, bf16[27,243]{1,0:T(8,128)(2,1)}, u32[]{:S(2)}) copy-start(bf16[27,243]{1,0:T(8,128)(2,1)} %constant.10.clone.refs_7_) | copy-start | bytes 39370
  4.7 0.7 %copy-start.5 = (s32[6,192]{1,0:T(8,128)S(1)}, s32[6,192]{1,0:T(8,128)}, u32[]{:S(2)}) copy-start(s32[6,192]{1,0:T(8,128)} %refs_3_.1) | copy-start | bytes 13828
  5.4 0.7 %copy-start.6 = (s32[6,192]{1,0:T(8,128)S(1)}, s32[6,192]{1,0:T(8,128)}, u32[]{:S(2)}) copy-start(s32[6,192]{1,0:T(8,128)} %refs_4_.1) | copy-start | bytes 13828
  6.1 0.7 %copy-start.7 = (s32[32]{0:T(128)S(1)}, s32[32]{0:T(128)}, u32[]{:S(2)}) copy-start(s32[32]{0:T(128)} %refs_2_.1) | copy-start | bytes 388

commit v2 on v1

--- a/solution.py
+++ b/solution.py
@@ -23,8 +23,8 @@
 
 def selections():
     send = np.zeros((6 * FACE_ROWS, ROWS), np.float32)
-    inside = np.zeros((72, NODES), np.float32)
-    lift = np.zeros((NODES, 72), np.float32)
+    inside = np.zeros((80, NODES), np.float32)
+    lift = np.zeros((32, 72), np.float32)
     for face in range(6):
         for position in range(9):
             node = face_node(face, position)
@@ -41,6 +41,7 @@
         ],
         axis=1,
     ).astype(np.float32)
+    along = np.pad(along, ((0, 5), (0, 0)))
     thrice = lambda m: np.concatenate([m, m, m], axis=1)
     return [jnp.asarray(thrice(m), jnp.bfloat16) for m in (send, inside, along, lift)]
 
@@ -66,13 +67,13 @@
 
 def kernel(
     n_gx, n_gy,
-    state_ref, inverse_ref, start_ref, neigh_ref, orient_ref,
-    send_mat, inside_mat, along_mat, lift_mat,
+    state_hbm, inverse_ref, start_hbm, neigh_hbm, orient_hbm, send_hbm, inside_hbm, along_hbm, lift_hbm,
     new_ref, residual_ref,
+    state_ref, start_ref, neigh_ref, orient_ref, send_mat, inside_mat, along_mat, lift_mat,
     block_ref, view_ref, edge_prev, edge_next,
-    traces_ref, far_ref, out_ref, res_ref, res_prev, res_next,
+    raw_ref, traces_ref, far_ref, far_prev, far_next, out_ref, res_ref, res_prev, res_next,
     old_res, upd_ref, upd_prev, upd_next, index_ref, code_ref,
-    load_sem, send_sem, recv_sem,
+    input_sem, load_sem, send_sem, recv_sem,
 ):
     elems = neigh_ref.shape[1]
     capacity = state_ref.shape[1]
@@ -84,18 +85,48 @@
 
     after = lax.rem(me + 1, count)
     before = lax.rem(me + count - 1, count)
-    nxt = (after // n_gy, lax.rem(after, n_gy))
-    prv = (before // n_gy, lax.rem(before, n_gy))
-    sides = [
-        (lax.rem(gx + n_gx - 1, n_gx), gy),
-        (lax.rem(gx + 1, n_gx), gy),
-        (gx, lax.rem(gy + n_gy - 1, n_gy)),
-        (gx, lax.rem(gy + 1, n_gy)),
-    ]
+    def coords(device):
+        return (device // n_gy, lax.rem(device, n_gy))
+
+    def side(face, device):
+        x, y = coords(device)
+        step = 1 if face % 2 else -1
+        if face < 2:
+            x = lax.rem(x + n_gx + step, n_gx)
+        else:
+            y = lax.rem(y + n_gy + step, n_gy)
+        return x * n_gy + y
+
+    nxt, prv = coords(after), coords(before)
+    sides = [side(face, me) for face in range(4)]
+    via_next = [side(face, after) for face in range(4)]
+    via_prev = [side(face, before) for face in range(4)]
+
+    inputs = []
+    for slot, (source, target) in enumerate(
+        [
+            (state_hbm, state_ref), (start_hbm, start_ref), (send_hbm, send_mat),
+            (neigh_hbm, neigh_ref), (orient_hbm, orient_ref), (inside_hbm, inside_mat),
+            (along_hbm, along_mat), (lift_hbm, lift_mat),
+        ]
+    ):
+        load = pltpu.make_async_copy(source, target, input_sem.at[slot])
+        load.start()
+        inputs.append(load)
 
     barrier = pltpu.get_barrier_semaphore()
-    for device in [nxt, prv] + sides:
-        pl.semaphore_signal(barrier, inc=1, device_id=device, device_id_type=MESH)
+    for device in [after, before] + sides:
+        pl.semaphore_signal(barrier, inc=1, device_id=coords(device), device_id_type=MESH)
+    expected = 6
+    for face in range(4):
+        for sender in (
+            lax.rem(sides[face] + count - 1, count), lax.rem(sides[face] + 1, count)
+        ):
+            expected = expected + jnp.where(sender == me, 0, 1)
+
+            @pl.when(sender != me)
+            def _():
+                pl.semaphore_signal(barrier, inc=1, device_id=coords(sender), device_id_type=MESH)
 
     rows = ROWS // CHUNKS
     loads = []
@@ -115,18 +146,51 @@
         copy.start()
         return copy
 
-    start = start_ref[me]
-    end = jnp.where(me == count - 1, count * elems, start_ref[lax.rem(me + 1, count)])
-    held = end - start
-    shift = me * elems - start
+    def post(slot, source, target, device):
+        remote = pltpu.make_async_remote_copy(
+            src_ref=source, dst_ref=target, send_sem=send_sem.at[slot],
+            recv_sem=recv_sem.at[slot], device_id=coords(device), device_id_type=MESH,
+        )
+        local = pltpu.make_async_copy(source, target, recv_sem.at[slot])
+        pl.when(device != me)(remote.start)
+        pl.when(device == me)(local.start)
+        return device, remote, local
+
+    def arrive(posted):
+        device, remote, local = posted
+        pl.when(device != me)(remote.wait)
+        pl.when(device == me)(local.wait)
+
+    def range_of(device):
+        start = start_ref[device]
+        end = jnp.where(
+            device == count - 1, count * elems, start_ref[lax.rem(device + 1, count)]
+        )
+        return device * elems - start, end - start
+
+    for load in inputs[:3]:
+        load.wait()
+    shift, held = range_of(me)
     to_new = jnp.where(shift > 0, capacity - shift, -shift)
     to_old = jnp.where(shift >= 0, shift, capacity + shift)
 
     view_ref[...] = pltpu.roll(state_ref[...], to_new, 1)
-    pl.semaphore_wait(barrier, 6)
+    raw_ref[...] = times(send_mat[pl.ds(0, 4 * FACE_ROWS), :], view_ref[...])
+    pl.semaphore_wait(barrier, expected)
     edge = view_ref.at[:, pl.ds(half, half)]
+    posted = []
+    for face in range(4):
+        where = pl.ds(face * FACE_ROWS, FACE_ROWS)
+        ends = raw_ref.at[where, pl.ds(half, half)]
+        posted.append(post(6 + face, ends, far_prev.at[where], via_next[face]))
+        posted.append(post(10 + face, ends, far_next.at[where], via_prev[face]))
     copies = [send(0, edge, edge_prev, nxt), send(1, edge, edge_next, prv)]
-
+    for face in range(4):
+        where = pl.ds(face * FACE_ROWS, FACE_ROWS)
+        copies.append(send(2 + face, raw_ref.at[where], far_ref.at[where], coords(sides[face])))
+
+    for load in inputs[3:]:
+        load.wait()
     index_ref[...] = jnp.zeros_like(index_ref)
     code_ref[...] = jnp.zeros_like(code_ref)
     index_ref[0:6, 0:elems] = neigh_ref[...]
@@ -136,40 +200,27 @@
         local = index_ref[face : face + 1, :] - me * elems
         if face < 4:
             own = jnp.logical_and(local >= 0, local < elems)
-            other = sides[face][0] * n_gy + sides[face][1]
-            local = jnp.where(own, local, capacity + local + (me - other) * elems)
+            local = jnp.where(own, local, capacity + local + (me - sides[face]) * elems)
         width = capacity * (2 if face < 4 else 1)
         columns = lax.broadcasted_iota(jnp.int32, (width, capacity), 0)
         choices.append(jnp.where(columns == local, 1.0, 0.0).astype(jnp.bfloat16))
 
     lane = lax.broadcasted_iota(jnp.int32, (1, half), 1)
 
-    def merged(ref, from_prev, from_next):
-        low = jnp.where(lane + shift < 0, pltpu.roll(from_prev[...], half // 2, 1), ref[:, 0:half])
-        high = jnp.where(
-            lane + half + shift >= held, pltpu.roll(from_next[...], half // 2, 1), ref[:, half:]
-        )
+    def merged(low, high, from_prev, from_next, shift, held):
+        low = jnp.where(lane + shift < 0, pltpu.roll(from_prev, half // 2, 1), low)
+        high = jnp.where(lane + half + shift >= held, pltpu.roll(from_next, half // 2, 1), high)
         return low, high
 
-    for copy in copies:
+    for copy in copies[:2]:
         copy.wait()
-    low, high = merged(view_ref, edge_prev, edge_next)
-    high = jnp.where(lane + half < elems, high, 0.0)
+    low, high = merged(
+        view_ref[:, 0:half], view_ref[:, half:], edge_prev[...], edge_next[...], shift, held
+    )
     view_ref[:, 0:half] = low
     view_ref[:, half:] = high
     state = view_ref[...]
-
     traces_ref[...] = times(send_mat[...], state)
-    copies = []
-    for face in range(4):
-        copies.append(
-            send(
-                2 + face,
-                traces_ref.at[pl.ds(face * FACE_ROWS, FACE_ROWS)],
-                far_ref.at[pl.ds(face * FACE_ROWS, FACE_ROWS)],
-                sides[face],
-            )
-        )
 
     u = [view_ref[NODES * v : NODES * (v + 1), :] for v in range(5)]
     inverse_density = 1.0 / u[0]
@@ -182,18 +233,24 @@
             value = u[1 + j] * velocity
             flux[1 + j].append(value + pressure if j == k else value)
         flux[4].append((u[4] + pressure) * velocity)
-    volume = [times(along_mat[...], jnp.concatenate(flux[v], axis=0)) for v in range(5)]
-    inside = [times(inside_mat[...], u[v]).reshape(9, 8, capacity) for v in range(5)]
-
-    for face in range(4):
-        copies[face].wait()
+    volume = [times(along_mat[...], jnp.concatenate(flux[v], axis=0))[0:NODES] for v in range(5)]
+    inside = [times(inside_mat[...], u[v])[0:72].reshape(9, 8, capacity) for v in range(5)]
+
+    for copy in copies[2:]:
+        copy.wait()
+    for item in posted:
+        arrive(item)
 
     out_ref[...] = jnp.zeros_like(out_ref)
     for face in range(6):
         where = pl.ds((face ^ 1) * FACE_ROWS, FACE_ROWS)
         block = traces_ref[where, :]
         if face < 4:
-            block = jnp.concatenate([block, far_ref[where, :]], axis=1)
+            low, high = merged(
+                far_ref[where, 0:half], far_ref[where, half:], far_prev[where, :],
+                far_next[where, :], *range_of(sides[face]),
+            )
+            block = jnp.concatenate([block, low, high], axis=1)
         pieces = jnp.dot(
             jnp.concatenate(parts_of(block), axis=0), choices[face],
             preferred_element_type=jnp.float32,
@@ -235,11 +292,11 @@
     for v in range(5):
         term = 1.5 * (outward * (flux_out[v] - flux_in[v]) - speed * (outside[v] - inside[v]))
         term = jnp.where(real, term, 0.0).reshape(72, capacity)
-        res_ref[NODES * v : NODES * (v + 1), :] = volume[v] + times(lift_mat[...], term)
+        res_ref[NODES * v : NODES * (v + 1), :] = volume[v] + times(lift_mat[...], term)[0:NODES]
 
     copies = [
-        send(6, res_ref.at[:, pl.ds(0, half)], res_next, prv),
-        send(7, res_ref.at[:, pl.ds(half, half)], res_prev, nxt),
+        send(14, res_ref.at[:, pl.ds(0, half)], res_next, prv),
+        send(15, res_ref.at[:, pl.ds(half, half)], res_prev, nxt),
     ]
     residual_ref[...] = res_ref[:, 0:elems]
     for copy in copies:
@@ -267,10 +324,12 @@
 
     upd_ref[...] = pltpu.roll(upd_ref[...], to_new, 1)
     edge = upd_ref.at[:, pl.ds(half, half)]
-    copies = [send(8, edge, upd_prev, nxt), send(9, edge, upd_next, prv)]
+    copies = [send(16, edge, upd_prev, nxt), send(17, edge, upd_next, prv)]
     for copy in copies:
         copy.wait()
-    low, high = merged(upd_ref, upd_prev, upd_next)
+    low, high = merged(
+        upd_ref[:, 0:half], upd_ref[:, half:], upd_prev[...], upd_next[...], shift, held
+    )
     new_ref[:, 0:half] = view_ref[:, 0:half] - low
     new_ref[:, half:elems] = (view_ref[:, half:] - high)[:, 0 : elems - half]
 
@@ -281,36 +340,38 @@
     def body(old_state, old_inverse, old_start, neighbours, orientation):
         elems, capacity = neighbours.shape[1], old_state.shape[1]
         half = capacity // 2
+        matrices = selections()
         vmem = pl.BlockSpec(memory_space=pltpu.VMEM)
         f32 = lambda *shape: pltpu.VMEM(shape, jnp.float32)
         call = pl.pallas_call(
             lambda *refs: kernel(n_gx, n_gy, *refs),
             out_shape=[jax.ShapeDtypeStruct((ROWS, elems), jnp.float32)] * 2,
-            in_specs=[
-                vmem,
-                pl.BlockSpec(memory_space=pl.ANY),
-                pl.BlockSpec(memory_space=pltpu.SMEM),
-                vmem, vmem, vmem, vmem, vmem, vmem,
-            ],
+            in_specs=[pl.BlockSpec(memory_space=pltpu.HBM)] * 9,
             out_specs=[vmem, vmem],
             scratch_shapes=[
+                f32(ROWS, capacity),
+                pltpu.SMEM(old_start.shape, jnp.int32),
+                pltpu.VMEM((6, elems), jnp.int32), pltpu.VMEM((6, elems), jnp.int32),
+                *[pltpu.VMEM(m.shape, m.dtype) for m in matrices],
                 pltpu.VMEM((ROWS, ROWS, capacity), jnp.bfloat16),
                 f32(ROWS, capacity), f32(ROWS, half), f32(ROWS, half),
-                f32(6 * FACE_ROWS, capacity), f32(4 * FACE_ROWS, capacity),
+                f32(4 * FACE_ROWS, capacity), f32(6 * FACE_ROWS, capacity),
+                f32(4 * FACE_ROWS, capacity), f32(4 * FACE_ROWS, half), f32(4 * FACE_ROWS, half),
                 f32(45, 8, capacity),
                 f32(ROWS, capacity), f32(ROWS, half), f32(ROWS, half),
                 f32(ROWS, capacity),
                 f32(ROWS, capacity), f32(ROWS, half), f32(ROWS, half),
                 pltpu.VMEM((8, capacity), jnp.int32), pltpu.VMEM((8, capacity), jnp.int32),
+                pltpu.SemaphoreType.DMA((8,)),
                 pltpu.SemaphoreType.DMA((CHUNKS,)),
-                pltpu.SemaphoreType.DMA((10,)),
-                pltpu.SemaphoreType.DMA((10,)),
+                pltpu.SemaphoreType.DMA((18,)),
+                pltpu.SemaphoreType.DMA((18,)),
             ],
             compiler_params=pltpu.CompilerParams(
                 collective_id=0, has_side_effects=True, vmem_limit_bytes=48 * 1024 * 1024
             ),
         )
-        return tuple(call(old_state, old_inverse, old_start, neighbours, orientation, *selections()))
+        return tuple(call(old_state, old_inverse, old_start, neighbours, orientation, *matrices))
 
     spread = P(None, ("gx", "gy"))
     return jax.shard_map(

time: 39 us -> 37.6 us (0.964)
  Pallas kernels: 30.5 us -> 29.1 us
    pallas_call x1, Pallas kernels: 30.5 us -> 29.1 us  [body(): call(old_state, old_inverse, old_start, neighbours, orientation, *matrices)]
where the time goes in v2:
time: 37.6 us; the launch traced here: 37.1 us
  Pallas kernels  29.1 us (77%)
  local copies, waits for them, and re-layouts  7.39 us (20%)
  between operations  0.66 us (2%)
    pallas_call x1, Pallas kernels, body(): call(old_state, old_inverse, old_start, neighbours, orientation, *matrices)  29.1 us
    unnamed x18, local copies, waits for them, and re-layouts  7.39 us

profile of v2, /device:TPU:0, one launch (start us, length us, event | category | flops | bytes accessed | tf_op | source)
XLA Modules:
  0.0 37.1 jit_solution(16183332720113359821)
XLA Ops:
  0.6 0.0 copy-start
  0.6 1.0 %copy-done = bf16[288,405]{1,0:T(8,128)(2,1)S(1)} copy-done((bf16[288,405]{1,0:T(8,128)(2,1)S(1)}, bf16[288,405]{1,0:T(8,128)(2,1)}, u32[]{:S(2)}) %copy-start) | copy-done | bytes 233304
  1.6 0.0 copy-start.1
  1.6 0.9 %copy-done.1 = f32[135,256]{1,0:T(8,128)S(1)} copy-done((f32[135,256]{1,0:T(8,128)S(1)}, f32[135,256]{1,0:T(8,128)}, u32[]{:S(2)}) %copy-start.1) | copy-done | bytes 138264
  2.5 0.0 copy-start.2
  2.5 0.7 %copy-done.2 = bf16[80,81]{1,0:T(8,128)(2,1)S(1)} copy-done((bf16[80,81]{1,0:T(8,128)(2,1)S(1)}, bf16[80,81]{1,0:T(8,128)(2,1)}, u32[]{:S(2)}) %copy-start.2) | copy-done | bytes 12984
  3.2 0.0 copy-start.3
  3.2 0.7 %copy-done.3 = bf16[32,216]{1,0:T(8,128)(2,1)S(1)} copy-done((bf16[32,216]{1,0:T(8,128)(2,1)S(1)}, bf16[32,216]{1,0:T(8,128)(2,1)}, u32[]{:S(2)}) %copy-start.3) | copy-done | bytes 13848
  3.9 0.0 copy-start.4
  4.0 0.7 %copy-done.4 = bf16[32,243]{1,0:T(8,128)(2,1)S(1)} copy-done((bf16[32,243]{1,0:T(8,128)(2,1)S(1)}, bf16[32,243]{1,0:T(8,128)(2,1)}, u32[]{:S(2)}) %copy-start.4) | copy-done | bytes 15576
  4.7 0.0 copy-start.5
  4.7 0.7 %copy-done.5 = s32[6,192]{1,0:T(8,128)S(1)} copy-done((s32[6,192]{1,0:T(8,128)S(1)}, s32[6,192]{1,0:T(8,128)}, u32[]{:S(2)}) %copy-start.5) | copy-done | bytes 4632
  5.4 0.0 copy-start.6
  5.4 0.7 %copy-done.6 = s32[6,192]{1,0:T(8,128)S(1)} copy-done((s32[6,192]{1,0:T(8,128)S(1)}, s32[6,192]{1,0:T(8,128)}, u32[]{:S(2)}) %copy-start.6) | copy-done | bytes 4632
  6.1 0.0 copy-start.7
  6.1 0.7 %copy-done.7 = s32[32]{0:T(128)S(1)} copy-done((s32[32]{0:T(128)S(1)}, s32[32]{0:T(128)}, u32[]{:S(2)}) %copy-start.7) | copy-done | bytes 152
  6.7 29.1 %shard_map.104 = (f32[135,192]{1,0:T(8,128)S(1)}, f32[135,192]{1,0:T(8,128)S(1)}) custom-call(f32[135,256]{1,0:T(8,128)S(1)} %copy-done.1, bf16[135,135,256]{2,1,0:T(8,128)(2,1)} %refs_1_.1, s32[32]{0:T(128)S(1)} %copy-done.7, s32[6,192]{1,0:T(8,128)S(1)} %copy-done.5, s32[6,192]{1,0:T(8,128)S(1)} %copy-done.6, bf16[288,405]{1,0:T(8,128)(2,1)S(1)} %copy-done, ...), custom_call_target="tpu_custom_call" | custom-call | tf_op jit(solution)/shard_map/pallas_call | solution.py:374
  35.8 0.7 %copy.13 = f32[135,192]{1,0:T(8,128)} copy(f32[135,192]{1,0:T(8,128)S(1)} %get-tuple-element.4) | data formatting | bytes 207360
  36.5 0.7 %copy.14 = f32[135,192]{1,0:T(8,128)} copy(f32[135,192]{1,0:T(8,128)S(1)} %get-tuple-element.5) | data formatting | bytes 207360
Async XLA Ops:
  0.6 1.0 %copy-start = (bf16[288,405]{1,0:T(8,128)(2,1)S(1)}, bf16[288,405]{1,0:T(8,128)(2,1)}, u32[]{:S(2)}) copy-start(bf16[288,405]{1,0:T(8,128)(2,1)} %constant.8.clone.refs_5_) | copy-start | bytes 699844
  1.6 0.9 %copy-start.1 = (f32[135,256]{1,0:T(8,128)S(1)}, f32[135,256]{1,0:T(8,128)}, u32[]{:S(2)}) copy-start(f32[135,256]{1,0:T(8,128)} %refs_0_.1) | copy-start | bytes 414724
  2.5 0.7 %copy-start.2 = (bf16[80,81]{1,0:T(8,128)(2,1)S(1)}, bf16[80,81]{1,0:T(8,128)(2,1)}, u32[]{:S(2)}) copy-start(bf16[80,81]{1,0:T(8,128)(2,1)} %constant.9.clone.refs_6_) | copy-start | bytes 38884
  3.2 0.7 %copy-start.3 = (bf16[32,216]{1,0:T(8,128)(2,1)S(1)}, bf16[32,216]{1,0:T(8,128)(2,1)}, u32[]{:S(2)}) copy-start(bf16[32,216]{1,0:T(8,128)(2,1)} %constant.11.clone.refs_8_) | copy-start | bytes 41476
  3.9 0.7 %copy-start.4 = (bf16[32,243]{1,0:T(8,128)(2,1)S(1)}, bf16[32,243]{1,0:T(8,128)(2,1)}, u32[]{:S(2)}) copy-start(bf16[32,243]{1,0:T(8,128)(2,1)} %constant.10.clone.refs_7_) | copy-start | bytes 46660
  4.7 0.7 %copy-start.5 = (s32[6,192]{1,0:T(8,128)S(1)}, s32[6,192]{1,0:T(8,128)}, u32[]{:S(2)}) copy-start(s32[6,192]{1,0:T(8,128)} %refs_3_.1) | copy-start | bytes 13828
  5.4 0.7 %copy-start.6 = (s32[6,192]{1,0:T(8,128)S(1)}, s32[6,192]{1,0:T(8,128)}, u32[]{:S(2)}) copy-start(s32[6,192]{1,0:T(8,128)} %refs_4_.1) | copy-start | bytes 13828
  6.1 0.7 %copy-start.7 = (s32[32]{0:T(128)S(1)}, s32[32]{0:T(128)}, u32[]{:S(2)}) copy-start(s32[32]{0:T(128)} %refs_2_.1) | copy-start | bytes 388

commit v3 on v2

--- a/solution.py
+++ b/solution.py
@@ -12,6 +12,8 @@
 ROWS = 135
 FACE_ROWS = 48
 CHUNKS = 5
+TALL = 160
+EDGE = 32
 
 
 def face_node(face, position):
@@ -60,6 +62,24 @@
     )
 
 
+def packed(x, first, height):
+    lane = lax.broadcasted_iota(jnp.int32, (1, 128), 1)
+    result = jnp.zeros((height, 128), x.dtype)
+    for group in range(x.shape[0] // height):
+        rolled = pltpu.roll(
+            x[group * height : (group + 1) * height], (group * EDGE - first) % 128, 1
+        )
+        inside = jnp.logical_and(lane >= group * EDGE, lane < (group + 1) * EDGE)
+        result = jnp.where(inside, rolled, result)
+    return result
+
+
+def unpacked(x, first, groups):
+    return jnp.concatenate(
+        [pltpu.roll(x, (first - group * EDGE) % 128, 1) for group in range(groups)], axis=0
+    )
+
+
 def pressure_of(u, inverse_density):
     kinetic = (u[1] * u[1] + u[2] * u[2] + u[3] * u[3]) * inverse_density
     return 0.4 * (u[4] - 0.5 * kinetic)
@@ -70,7 +90,7 @@
     state_hbm, inverse_ref, start_hbm, neigh_hbm, orient_hbm, send_hbm, inside_hbm, along_hbm, lift_hbm,
     new_ref, residual_ref,
     state_ref, start_ref, neigh_ref, orient_ref, send_mat, inside_mat, along_mat, lift_mat,
-    block_ref, view_ref, edge_prev, edge_next,
+    block_ref, view_ref, to_prev, to_next, edge_prev, edge_next, raw_prev, raw_next,
     raw_ref, traces_ref, far_ref, far_prev, far_next, out_ref, res_ref, res_prev, res_next,
     old_res, upd_ref, upd_prev, upd_next, index_ref, code_ref,
     input_sem, load_sem, send_sem, recv_sem,
@@ -174,20 +194,26 @@
     to_new = jnp.where(shift > 0, capacity - shift, -shift)
     to_old = jnp.where(shift >= 0, shift, capacity + shift)
 
-    view_ref[...] = pltpu.roll(state_ref[...], to_new, 1)
-    raw_ref[...] = times(send_mat[pl.ds(0, 4 * FACE_ROWS), :], view_ref[...])
+    for ref in (view_ref, res_ref, upd_ref):
+        ref[ROWS:, :] = jnp.zeros((TALL - ROWS, capacity), jnp.float32)
+    view_ref[0:ROWS, :] = pltpu.roll(state_ref[...], to_new, 1)
+    to_next[0] = packed(view_ref[:, half:], half // 2, TALL // 4)
+    to_prev[0] = packed(view_ref[:, half:], half // 2 + EDGE, TALL // 4)
+    raw_ref[...] = times(send_mat[pl.ds(0, 4 * FACE_ROWS), :], view_ref[0:ROWS, :])
+    for face in range(4):
+        ends = raw_ref[face * FACE_ROWS : (face + 1) * FACE_ROWS, half:]
+        raw_next[face * 16 : face * 16 + 16, :] = packed(ends, half // 2, 16)
+        raw_prev[face * 16 : face * 16 + 16, :] = packed(ends, half // 2 + EDGE, 16)
     pl.semaphore_wait(barrier, expected)
-    edge = view_ref.at[:, pl.ds(half, half)]
     posted = []
-    for face in range(4):
-        where = pl.ds(face * FACE_ROWS, FACE_ROWS)
-        ends = raw_ref.at[where, pl.ds(half, half)]
-        posted.append(post(6 + face, ends, far_prev.at[where], via_next[face]))
-        posted.append(post(10 + face, ends, far_next.at[where], via_prev[face]))
-    copies = [send(0, edge, edge_prev, nxt), send(1, edge, edge_next, prv)]
+    copies = [send(0, to_next.at[0], edge_prev, nxt), send(1, to_prev.at[0], edge_next, prv)]
     for face in range(4):
         where = pl.ds(face * FACE_ROWS, FACE_ROWS)
         copies.append(send(2 + face, raw_ref.at[where], far_ref.at[where], coords(sides[face])))
+    for face in range(4):
+        where = pl.ds(face * 16, 16)
+        posted.append(post(6 + face, raw_next.at[where], far_prev.at[where], via_next[face]))
+        posted.append(post(10 + face, raw_prev.at[where], far_next.at[where], via_prev[face]))
 
     for load in inputs[3:]:
         load.wait()
@@ -208,8 +234,11 @@
     lane = lax.broadcasted_iota(jnp.int32, (1, half), 1)
 
     def merged(low, high, from_prev, from_next, shift, held):
-        low = jnp.where(lane + shift < 0, pltpu.roll(from_prev, half // 2, 1), low)
-        high = jnp.where(lane + half + shift >= held, pltpu.roll(from_next, half // 2, 1), high)
+        groups = -(-low.shape[0] // from_prev.shape[0])
+        first = unpacked(from_prev, 0, groups)[0 : low.shape[0]]
+        last = unpacked(from_next, elems - half - EDGE, groups)[0 : low.shape[0]]
+        low = jnp.where(lane + shift < 0, first, low)
+        high = jnp.where(lane + half + shift >= held, last, high)
         return low, high
 
     for copy in copies[:2]:
@@ -219,8 +248,7 @@
     )
     view_ref[:, 0:half] = low
     view_ref[:, half:] = high
-    state = view_ref[...]
-    traces_ref[...] = times(send_mat[...], state)
+    traces_ref[...] = times(send_mat[...], view_ref[0:ROWS, :])
 
     u = [view_ref[NODES * v : NODES * (v + 1), :] for v in range(5)]
     inverse_density = 1.0 / u[0]
@@ -244,11 +272,12 @@
     out_ref[...] = jnp.zeros_like(out_ref)
     for face in range(6):
         where = pl.ds((face ^ 1) * FACE_ROWS, FACE_ROWS)
+        edge = pl.ds((face ^ 1) * 16, 16)
         block = traces_ref[where, :]
         if face < 4:
             low, high = merged(
-                far_ref[where, 0:half], far_ref[where, half:], far_prev[where, :],
-                far_next[where, :], *range_of(sides[face]),
+                far_ref[where, 0:half], far_ref[where, half:], far_prev[edge, :],
+                far_next[edge, :], *range_of(sides[face]),
             )
             block = jnp.concatenate([block, low, high], axis=1)
         pieces = jnp.dot(
@@ -294,21 +323,23 @@
         term = jnp.where(real, term, 0.0).reshape(72, capacity)
         res_ref[NODES * v : NODES * (v + 1), :] = volume[v] + times(lift_mat[...], term)[0:NODES]
 
-    copies = [
-        send(14, res_ref.at[:, pl.ds(0, half)], res_next, prv),
-        send(15, res_ref.at[:, pl.ds(half, half)], res_prev, nxt),
-    ]
-    residual_ref[...] = res_ref[:, 0:elems]
+    to_prev[1] = packed(res_ref[:, 0:half], 0, TALL // 4)
+    to_next[1] = packed(res_ref[:, half:], elems - half - EDGE, TALL // 4)
+    copies = [send(14, to_prev.at[1], res_next, prv), send(15, to_next.at[1], res_prev, nxt)]
+    residual_ref[...] = res_ref[0:ROWS, 0:elems]
     for copy in copies:
         copy.wait()
-    quarter = half // 2
-    inner = lane < elems - half
-    to_next = lane < elems - half + quarter // 2
     high = jnp.where(
-        inner, res_ref[:, half:],
-        jnp.where(to_next, pltpu.roll(res_next[...], quarter, 1), pltpu.roll(res_prev[...], quarter, 1)),
-    )
-    old_res[...] = pltpu.roll(jnp.concatenate([res_ref[:, 0:half], high], axis=1), to_old, 1)
+        lane < elems - half, res_ref[0:ROWS, half:],
+        jnp.where(
+            lane < elems - half + EDGE,
+            unpacked(res_next[...], elems - half, 4)[0:ROWS],
+            unpacked(res_prev[...], elems - half + EDGE, 4)[0:ROWS],
+        ),
+    )
+    old_res[...] = pltpu.roll(
+        jnp.concatenate([res_ref[0:ROWS, 0:half], high], axis=1), to_old, 1
+    )
 
     for chunk in range(CHUNKS):
         loads[chunk].wait()
@@ -322,16 +353,17 @@
 
         lax.fori_loop(0, rows // 3, apply, 0)
 
-    upd_ref[...] = pltpu.roll(upd_ref[...], to_new, 1)
-    edge = upd_ref.at[:, pl.ds(half, half)]
-    copies = [send(16, edge, upd_prev, nxt), send(17, edge, upd_next, prv)]
+    upd_ref[0:ROWS, :] = pltpu.roll(upd_ref[0:ROWS, :], to_new, 1)
+    to_next[2] = packed(upd_ref[:, half:], half // 2, TALL // 4)
+    to_prev[2] = packed(upd_ref[:, half:], half // 2 + EDGE, TALL // 4)
+    copies = [send(16, to_next.at[2], upd_prev, nxt), send(17, to_prev.at[2], upd_next, prv)]
     for copy in copies:
         copy.wait()
     low, high = merged(
         upd_ref[:, 0:half], upd_ref[:, half:], upd_prev[...], upd_next[...], shift, held
     )
-    new_ref[:, 0:half] = view_ref[:, 0:half] - low
-    new_ref[:, half:elems] = (view_ref[:, half:] - high)[:, 0 : elems - half]
+    new_ref[:, 0:half] = (view_ref[:, 0:half] - low)[0:ROWS]
+    new_ref[:, half:elems] = (view_ref[:, half:] - high)[0:ROWS, 0 : elems - half]
 
 
 def solution(mesh):
@@ -354,13 +386,14 @@
                 pltpu.VMEM((6, elems), jnp.int32), pltpu.VMEM((6, elems), jnp.int32),
                 *[pltpu.VMEM(m.shape, m.dtype) for m in matrices],
                 pltpu.VMEM((ROWS, ROWS, capacity), jnp.bfloat16),
-                f32(ROWS, capacity), f32(ROWS, half), f32(ROWS, half),
+                f32(TALL, capacity), f32(3, TALL // 4, half), f32(3, TALL // 4, half),
+                f32(TALL // 4, half), f32(TALL // 4, half), f32(64, half), f32(64, half),
                 f32(4 * FACE_ROWS, capacity), f32(6 * FACE_ROWS, capacity),
-                f32(4 * FACE_ROWS, capacity), f32(4 * FACE_ROWS, half), f32(4 * FACE_ROWS, half),
+                f32(4 * FACE_ROWS, capacity), f32(64, half), f32(64, half),
                 f32(45, 8, capacity),
-                f32(ROWS, capacity), f32(ROWS, half), f32(ROWS, half),
+                f32(TALL, capacity), f32(TALL // 4, half), f32(TALL // 4, half),
                 f32(ROWS, capacity),
-                f32(ROWS, capacity), f32(ROWS, half), f32(ROWS, half),
+                f32(TALL, capacity), f32(TALL // 4, half), f32(TALL // 4, half),
                 pltpu.VMEM((8, capacity), jnp.int32), pltpu.VMEM((8, capacity), jnp.int32),
                 pltpu.SemaphoreType.DMA((8,)),
                 pltpu.SemaphoreType.DMA((CHUNKS,)),
@@ -368,7 +401,7 @@
                 pltpu.SemaphoreType.DMA((18,)),
             ],
             compiler_params=pltpu.CompilerParams(
-                collective_id=0, has_side_effects=True, vmem_limit_bytes=48 * 1024 * 1024
+                collective_id=0, has_side_effects=True, vmem_limit_bytes=63 * 1024 * 1024
             ),
         )
         return tuple(call(old_state, old_inverse, old_start, neighbours, orientation, *matrices))

time: 37.6 us -> 29 us (0.77)
  local copies, waits for them, and re-layouts: 7.39 us -> 3.15 us
  Pallas kernels: 29.1 us -> 25 us
    unnamed x18 -> x2, local copies, waits for them, and re-layouts: 7.39 us -> 3.15 us
    pallas_call x1, Pallas kernels: 29.1 us -> 25 us  [body(): call(old_state, old_inverse, old_start, neighbours, orientation, *matrices)]
where the time goes in v3:
time: 29 us; the launch traced here: 28.8 us
  Pallas kernels  25 us (86%)
  local copies, waits for them, and re-layouts  3.15 us (11%)
  between operations  0.64 us (2%)
    pallas_call x1, Pallas kernels, body(): call(old_state, old_inverse, old_start, neighbours, orientation, *matrices)  25 us
    unnamed x2, local copies, waits for them, and re-layouts  3.15 us

profile of v3, /device:TPU:0, one launch (start us, length us, event | category | flops | bytes accessed | tf_op | source)
XLA Modules:
  0.0 28.8 jit_solution(1429424881477413502)
XLA Ops:
  0.6 25.0 %shard_map.104 = (f32[135,192]{1,0:T(8,128)}, f32[135,192]{1,0:T(8,128)}) custom-call(f32[135,256]{1,0:T(8,128)} %refs_0_.1, bf16[135,135,256]{2,1,0:T(8,128)(2,1)} %refs_1_.1, s32[32]{0:T(128)} %refs_2_.1, s32[6,192]{1,0:T(8,128)} %refs_3_.1, s32[6,192]{1,0:T(8,128)} %refs_4_.1, bf16[288,405]{1,0:T(8,128)(2,1)} %constant.8.clone.refs_5_, ...), custom_call_target="tpu_custom_call" | custom-call | tf_op jit(solution)/shard_map/pallas_call | solution.py:407
  25.7 1.6 %copy.13 = f32[135,192]{1,0:T(8,128)} copy(f32[135,192]{1,0:T(8,128)} %get-tuple-element.4) | data formatting | bytes 207360
  27.2 1.6 %copy.14 = f32[135,192]{1,0:T(8,128)} copy(f32[135,192]{1,0:T(8,128)} %get-tuple-element.5) | data formatting | bytes 207360

commit v4 on v3

--- a/solution.py
+++ b/solution.py
@@ -345,13 +345,13 @@
         loads[chunk].wait()
 
         def apply(step, carry):
-            for t in range(3):
-                row = chunk * rows + step * 3 + t
+            for t in range(9):
+                row = chunk * rows + step * 9 + t
                 product = block_ref[row].astype(jnp.float32) * old_res[...]
                 upd_ref[pl.ds(row, 1), :] = jnp.sum(product, axis=0, keepdims=True)
             return carry
 
-        lax.fori_loop(0, rows // 3, apply, 0)
+        lax.fori_loop(0, rows // 9, apply, 0)
 
     upd_ref[0:ROWS, :] = pltpu.roll(upd_ref[0:ROWS, :], to_new, 1)
     to_next[2] = packed(upd_ref[:, half:], half // 2, TALL // 4)

time: 29 us -> 28.5 us (0.983)
  Pallas kernels: 25 us -> 24.5 us
    pallas_call x1, Pallas kernels: 25 us -> 24.5 us  [body(): call(old_state, old_inverse, old_start, neighbours, orientation, *matrices)]
where the time goes in v4:
time: 28.5 us; the launch traced here: 28.3 us
  Pallas kernels  24.5 us (86%)
  local copies, waits for them, and re-layouts  3.15 us (11%)
  between operations  0.64 us (2%)
    pallas_call x1, Pallas kernels, body(): call(old_state, old_inverse, old_start, neighbours, orientation, *matrices)  24.5 us
    unnamed x2, local copies, waits for them, and re-layouts  3.15 us

profile of v4, /device:TPU:0, one launch (start us, length us, event | category | flops | bytes accessed | tf_op | source)
XLA Modules:
  0.0 28.3 jit_solution(5262113168605478570)
XLA Ops:
  0.6 24.5 %shard_map.104 = (f32[135,192]{1,0:T(8,128)}, f32[135,192]{1,0:T(8,128)}) custom-call(f32[135,256]{1,0:T(8,128)} %refs_0_.1, bf16[135,135,256]{2,1,0:T(8,128)(2,1)} %refs_1_.1, s32[32]{0:T(128)} %refs_2_.1, s32[6,192]{1,0:T(8,128)} %refs_3_.1, s32[6,192]{1,0:T(8,128)} %refs_4_.1, bf16[288,405]{1,0:T(8,128)(2,1)} %constant.8.clone.refs_5_, ...), custom_call_target="tpu_custom_call" | custom-call | tf_op jit(solution)/shard_map/pallas_call | solution.py:407
  25.2 1.6 %copy.13 = f32[135,192]{1,0:T(8,128)} copy(f32[135,192]{1,0:T(8,128)} %get-tuple-element.4) | data formatting | bytes 207360
  26.8 1.6 %copy.14 = f32[135,192]{1,0:T(8,128)} copy(f32[135,192]{1,0:T(8,128)} %get-tuple-element.5) | data formatting | bytes 207360
